TPU v7x, 32 devices: a whole 2x2x4 slice. The times are simulated.
32 devices in a mesh: dp: 4 (over x, core), ctx: 8 (over z, y).
Axes of the slice: x: 2, y: 2, z: 4, core: 2. Of those that a mesh axis runs over, the one named last changes fastest.
Arguments:
- queries: bfloat16 [4096, 4096], P(('dp', 'ctx')), may hold values from -6 to 6
- key_proj: bfloat16 [4096, 512], P(('dp', 'ctx')), may hold values from -6 to 6
- value_proj: bfloat16 [4096, 512], P(('dp', 'ctx')), may hold values from -6 to 6
- out_grad: bfloat16 [4096, 4096], P(('dp', 'ctx')), may hold values from -6 to 6
- row_plan: int32 [4096], P(('dp', 'ctx')), may hold values from 0 to 127, as said below
- segments: int32 [4, 1024], P('dp', 'ctx'), may hold values from 0 to 5, as said below
Outputs:
- attended: bfloat16 [4096, 4096], P(('dp', 'ctx'))
- query_grad: bfloat16 [4096, 4096], P(('dp', 'ctx'))
- key_grad: bfloat16 [4096, 512], P(('dp', 'ctx'))
- value_grad: bfloat16 [4096, 512], P(('dp', 'ctx'))
Inputs may be any that keep to these rules, and one draw needn't show every extreme that they name: `row_plan`: each aligned block of 128 entries (the rows of one device) is a permutation of 0 to 127. `segments`: along each row the ids never fall, and every id from 0 to 5 occurs. Every document has at most 640 positions, and in each row one document has exactly that many.
All inputs are finite; a program needn't handle non-finite values.
Results may differ from a plain program's by a relative error of at most 0.0083.
Values may be sent and summed in bfloat16 or wider, within the bound.
A program may use at most 128 MiB of HBM per device.

v0:
```python
import jax
import jax.numpy as jnp
from jax import lax
from jax.sharding import PartitionSpec as P

HEADS = 32
KV_HEADS = 4
HEAD_DIM = 128


NEG = -1e30


def passed_along(value, axis, steps):
    count = lax.axis_size(axis)
    first, last = (max(0, -steps), min(count, count - steps))
    return lax.ppermute(value, axis, [(source, source + steps) for source in range(first, last)])


def block_scores(q_heads, key_blk, seg_rows, pos_rows, seg_keys, pos_keys, scaling):
    raw_scores = (
        jnp.einsum("qkgd,skd->kgqs", q_heads, key_blk, preferred_element_type=jnp.float32) * scaling
    )
    visible = (seg_keys[None, :] == seg_rows[:, None]) & (pos_keys[None, :] <= pos_rows[:, None])
    return (jnp.where(visible, raw_scores, NEG), visible)


def on_device(queries, key_proj, value_proj, out_grad, row_plan, segments):
    rows_here = queries.shape[0]
    groups = HEADS // KV_HEADS
    scaling = HEAD_DIM ** (-0.5)
    inverse = jnp.zeros_like(row_plan).at[row_plan].set(jnp.arange(rows_here, dtype=jnp.int32))
    q_rows, k_rows, v_rows, d_rows = (
        lax.all_to_all(queries[row_plan], "dp", split_axis=0, concat_axis=0, tiled=True),
        lax.all_to_all(key_proj[row_plan], "dp", split_axis=0, concat_axis=0, tiled=True),
        lax.all_to_all(value_proj[row_plan], "dp", split_axis=0, concat_axis=0, tiled=True),
        lax.all_to_all(out_grad[row_plan], "dp", split_axis=0, concat_axis=0, tiled=True),
    )
    k_all, v_all, seg_all = (
        lax.all_gather(k_rows, "ctx", axis=0, tiled=True),
        lax.all_gather(v_rows, "ctx", axis=0, tiled=True),
        lax.all_gather(segments, "ctx", axis=1, tiled=True),
    )
    seq_len = k_all.shape[0]
    block_len = min(512, seq_len)
    blocks = seq_len // block_len
    my_index = lax.axis_index("ctx")
    first_row = my_index * rows_here
    last_row = first_row + rows_here - 1
    pos_rows = first_row + jnp.arange(rows_here, dtype=jnp.int32)
    seg_rows = segments[0]
    q_heads = q_rows.reshape(rows_here, KV_HEADS, groups, HEAD_DIM)

    def cut_block(keys_all, vals_all, seg_keys_all, block_idx):
        offset = block_idx * block_len
        key_blk = lax.dynamic_slice_in_dim(keys_all, offset, block_len, 0).reshape(
            block_len, KV_HEADS, HEAD_DIM
        )
        val_blk = lax.dynamic_slice_in_dim(vals_all, offset, block_len, 0).reshape(
            block_len, KV_HEADS, HEAD_DIM
        )
        seg_keys = lax.dynamic_slice_in_dim(seg_keys_all, offset, block_len, 0)
        pos_keys = offset + jnp.arange(block_len, dtype=jnp.int32)
        is_live = (offset <= last_row) & (seg_keys[block_len - 1] >= seg_rows[0])
        return (key_blk, val_blk, seg_keys, pos_keys, is_live, offset)

    seg_fwd = seg_all[0]

    def stats_step(block_idx, running):
        key_blk, val_blk, seg_keys, pos_keys, is_live, offset = cut_block(
            k_all, v_all, seg_fwd, block_idx
        )

        def stats_compute(running):
            row_top, row_sum = running
            scores, visible = block_scores(
                q_heads, key_blk, seg_rows, pos_rows, seg_keys, pos_keys, scaling
            )
            new_top = jnp.maximum(row_top, jnp.max(scores, axis=3))
            fresh = jnp.sum(jnp.where(visible, jnp.exp(scores - new_top[..., None]), 0.0), axis=3)
            return (new_top, row_sum * jnp.exp(row_top - new_top) + fresh)

        return lax.cond(is_live, stats_compute, lambda running: running, running)

    stat_shape = (KV_HEADS, groups, rows_here)
    row_top, row_sum = lax.fori_loop(
        0,
        blocks,
        stats_step,
        (jnp.full(stat_shape, NEG, jnp.float32), jnp.zeros(stat_shape, jnp.float32)),
    )
    log_sum = row_top + jnp.log(row_sum)

    def output_step(block_idx, running):
        key_blk, val_blk, seg_keys, pos_keys, is_live, offset = cut_block(
            k_all, v_all, seg_fwd, block_idx
        )

        def output_compute(running):
            scores, visible = block_scores(
                q_heads, key_blk, seg_rows, pos_rows, seg_keys, pos_keys, scaling
            )
            weights = jnp.where(visible, jnp.exp(scores - log_sum[..., None]), 0.0).astype(
                jnp.bfloat16
            )
            return running + jnp.einsum(
                "kgqs,skd->qkgd", weights, val_blk, preferred_element_type=jnp.float32
            )

        return lax.cond(is_live, output_compute, lambda running: running, running)

    out = lax.fori_loop(
        0, blocks, output_step, jnp.zeros((rows_here, KV_HEADS, groups, HEAD_DIM), jnp.float32)
    )
    back_out = lax.all_to_all(
        out.astype(jnp.bfloat16).reshape(rows_here, -1),
        "dp",
        split_axis=0,
        concat_axis=0,
        tiled=True,
    )
    attended = back_out[inverse]
    d_heads = d_rows.reshape(rows_here, KV_HEADS, groups, HEAD_DIM)
    row_dot = jnp.transpose(jnp.sum(d_heads.astype(jnp.float32) * out, axis=3), (1, 2, 0))
    back_k, back_v, back_seg = (
        lax.all_gather(k_rows, "ctx", axis=0, tiled=True),
        lax.all_gather(v_rows, "ctx", axis=0, tiled=True),
        lax.all_gather(segments, "ctx", axis=1, tiled=True),
    )
    seg_bwd = back_seg[0]

    def grad_step(block_idx, running):
        key_blk, val_blk, seg_keys, pos_keys, is_live, offset = cut_block(
            back_k, back_v, seg_bwd, block_idx
        )

        def grad_compute(running):
            q_grad, k_term, v_term = running
            scores, visible = block_scores(
                q_heads, key_blk, seg_rows, pos_rows, seg_keys, pos_keys, scaling
            )
            probs = jnp.where(visible, jnp.exp(scores - log_sum[..., None]), 0.0)
            weights = probs.astype(jnp.bfloat16)
            dprobs = jnp.einsum(
                "qkgd,skd->kgqs", d_heads, val_blk, preferred_element_type=jnp.float32
            )
            dscore = (probs * (dprobs - row_dot[..., None]) * scaling).astype(jnp.bfloat16)
            q_grad = q_grad + jnp.einsum(
                "kgqs,skd->qkgd", dscore, key_blk, preferred_element_type=jnp.float32
            )
            k_part = jnp.einsum(
                "kgqs,qkgd->skd", dscore, q_heads, preferred_element_type=jnp.float32
            )
            v_part = jnp.einsum(
                "kgqs,qkgd->skd", weights, d_heads, preferred_element_type=jnp.float32
            )
            k_term = lax.dynamic_update_slice_in_dim(k_term, k_part, offset, 0)
            v_term = lax.dynamic_update_slice_in_dim(v_term, v_part, offset, 0)
            return (q_grad, k_term, v_term)

        return lax.cond(is_live, grad_compute, lambda running: running, running)

    term_zeros = jnp.zeros((seq_len, KV_HEADS, HEAD_DIM), jnp.float32)
    q_grad, k_term, v_term = lax.fori_loop(
        0,
        blocks,
        grad_step,
        (jnp.zeros((rows_here, KV_HEADS, groups, HEAD_DIM), jnp.float32), term_zeros, term_zeros),
    )
    k_term = k_term.reshape(seq_len, -1)
    v_term = v_term.reshape(seq_len, -1)
    ctx_count = lax.axis_size("ctx")
    reach = min(ctx_count // 2 + 1, ctx_count - 1)

    def lower_slice(target):
        valid = (target >= 0).astype(jnp.float32)
        start = jnp.maximum(target, 0) * rows_here
        return (
            lax.dynamic_slice_in_dim(k_term, start, rows_here, 0) * valid,
            lax.dynamic_slice_in_dim(v_term, start, rows_here, 0) * valid,
        )

    def relay_step(step_count, carried):
        got_k, got_v = passed_along((carried[0], carried[1]), "ctx", -1)
        own_k, own_v = lower_slice(my_index - reach + step_count)
        return (got_k + own_k, got_v + own_v)

    k_owned, v_owned = lax.fori_loop(1, reach + 1, relay_step, lower_slice(my_index - reach))
    q_back, k_back, v_back = (
        lax.all_to_all(
            q_grad.astype(jnp.bfloat16).reshape(rows_here, -1),
            "dp",
            split_axis=0,
            concat_axis=0,
            tiled=True,
        ),
        lax.all_to_all(k_owned.astype(jnp.bfloat16), "dp", split_axis=0, concat_axis=0, tiled=True),
        lax.all_to_all(v_owned.astype(jnp.bfloat16), "dp", split_axis=0, concat_axis=0, tiled=True),
    )
    return (attended, q_back[inverse], k_back[inverse], v_back[inverse])


def solution(mesh):
    placed = (
        P(("dp", "ctx"), None),
        P(("dp", "ctx"), None),
        P(("dp", "ctx"), None),
        P(("dp", "ctx"), None),
        P(("dp", "ctx")),
        P("dp", "ctx"),
    )
    return jax.shard_map(
        on_device,
        mesh=mesh,
        in_specs=placed,
        out_specs=(
            P(("dp", "ctx"), None),
            P(("dp", "ctx"), None),
            P(("dp", "ctx"), None),
            P(("dp", "ctx"), None),
        ),
        check_vma=False,
    )
```

profile of v0, /device:TPU:0, one launch (start us, length us, event | category | flops | bytes accessed | tf_op | source)
XLA Modules:
  0.0 301.6 jit_solution(12016622625014973687)
XLA Ops:
  8.5 1.8 gather_fusion
  10.3 8.7 %all_to_all.90 = bf16[4,32,512]{2,1,0:T(8,128)(2,1)} all-to-all(bf16[4,32,512]{2,1,0:T(8,128)(2,1)S(1)} %bitcast.173), channel_id=1, replica_groups=mesh['dp'=4,'ctx'=8] {'dp'}, dimensions={0} | all-to-all | bytes 262144 | tf_op jit(solution)/shard_map/all_to_all | solution.py:35
  19.1 1.8 gather_fusion.2
  20.9 7.7 %all_to_all.91 = bf16[4,32,512]{2,1,0:T(8,128)(2,1)} all-to-all(bf16[4,32,512]{2,1,0:T(8,128)(2,1)S(1)} %bitcast.174), channel_id=1, replica_groups=mesh['dp'=4,'ctx'=8] {'dp'}, dimensions={0} | all-to-all | bytes 262144 | tf_op jit(solution)/shard_map/all_to_all | solution.py:36
  28.7 2.2 gather_fusion.4
  30.8 3.5 %all-to-all-start.4 = ((bf16[4,32,4096]{2,1,0:T(8,128)(2,1)}), bf16[4,32,4096]{2,1,0:T(8,128)(2,1)S(1)}, u32[]{:S(2)}, u32[]{:S(2)}) async-start(bf16[4,32,4096]{2,1,0:T(8,128)(2,1)} %bitcast.34), calls=%async_computation.4 | async-start | bytes 2097152 | tf_op jit(solution)/shard_map/all_to_all | solution.py:37
  34.4 2.2 gather_fusion.1
  36.5 12.2 %all-to-all-done.4 = bf16[4,32,4096]{2,1,0:T(8,128)(2,1)S(1)} async-done(((bf16[4,32,4096]{2,1,0:T(8,128)(2,1)}), bf16[4,32,4096]{2,1,0:T(8,128)(2,1)S(1)}, u32[]{:S(2)}, u32[]{:S(2)}) %all-to-all-start.4) | async-done | bytes 1048608 | tf_op jit(solution)/shard_map/all_to_all | solution.py:37
  48.8 3.5 %all-to-all-start.1 = ((bf16[4,32,4096]{2,1,0:T(8,128)(2,1)}), bf16[4,32,4096]{2,1,0:T(8,128)(2,1)S(1)}, u32[]{:S(2)}, u32[]{:S(2)}) async-start(bf16[4,32,4096]{2,1,0:T(8,128)(2,1)} %bitcast.30), calls=%async_computation.1 | async-start | bytes 2097152 | tf_op jit(solution)/shard_map/all_to_all | solution.py:34
  52.3 21.3 %all_gather.12 = s32[1,1024]{1,0:T(1,128)S(1)} all-gather(s32[1,128]{1,0:T(1,128)S(1)} %copy-done.10), channel_id=1, replica_groups=mesh['dp'=4,'ctx'=8] {'ctx'}, dimensions={1}, use_global_device_ids=true | all-gather | bytes 4608 | tf_op jit(solution)/shard_map/all_gather | solution.py:42
  78.6 6.9 %while.69 = (s32[]{:T(128)}, f32[4,8,128]{2,1,0:T(8,128)S(1)}, f32[4,8,128]{2,1,0:T(8,128)S(1)}, s32[]{:T(128)}, s32[1024]{0:T(1024)S(1)}, /*index=5*/s32[128]{0...) while((s32[]{:T(128)}, f32[4,8,128]{2,1,0:T(8,128)S(1)}, ...), condition=%wide.region_5.6_spmd.clone, body=%wide.region_0.5_spmd.clone.sunk | while | flops 553853568 | bytes 19825508 | solution.py:86
  80.1 3.9 %conditional.9 = ((f32[4,8,128]{2,1,0:T(8,128)S(1)}, f32[4,8,128]{2,1,0:T(8,128)S(1)})) conditional(s32[]{:T(128)} %convert_element_type.89, (f32[4,8,128]{2,1,0:T(8,128)S(1)}, f32[4,8,128]{2,1,0:T(8,128)S(1)}) %tuple.183, (s32[512]{0:T(512)S(1)}, s32[1,128]{1,0:T(1,128)S(1)}, s32[]{:T(128)}, s32[512]{0:T(512)S(1)}, s32[]{:T(128)}, ...), branch_computations={%region_1.1_spmd, %region_2.4_spmd} | conditional | flops 553853568 | bytes 19818532 | solution.py:83
  81.9 2.1 select_reduce_fusion
  85.6 15.7 %all-gather.5.cloned.1.call-done = bf16[1024,512]{1,0:T(8,128)(2,1)} async-done(((bf16[128,512]{1,0:T(8,128)(2,1)}), bf16[1024,512]{1,0:T(8,128)(2,1)}) %all-gather.5.cloned.1.call-update) | async-done | bytes 1048592 | tf_op jit(solution)/shard_map/all_gather | solution.py:41
  101.2 2.3 copy.95
  105.1 12.2 %while.70 = (s32[]{:T(128)}, f32[128,4,8,128]{3,0,2,1:T(8,128)}, s32[]{:T(128)}, s32[1024]{0:T(1024)S(1)}, s32[128]{0:T(128)S(1)}, /*index=5*/s32[1,128]{1,0:T(1...) while((s32[]{:T(128)}, f32[128,4,8,128]{3,0,2,1:T(8,128)}, ...), condition=%wide.region_9.0_spmd.clone, body=%wide.region_6.9_spmd.clone.sunk | while | flops 1084949120 | bytes 8553301 | solution.py:112
  106.5 9.4 %conditional.10 = (f32[128,4,8,128]{3,0,2,1:T(8,128)}) conditional(s32[]{:T(128)} %convert_element_type.90, f32[128,4,8,128]{3,0,2,1:T(8,128)} %get-tuple-element.1770, (s32[512]{0:T(512)S(1)}, s32[1,128]{1,0:T(1,128)S(1)}, s32[]{:T(128)}, s32[512]{0:T(512)S(1)}, s32[]{:T(128)}, /*index=5*/bf16[1024,512]{0,1:T(8,128)(2,1)S(1)}, s32[]{:T(128)}, ...), branch_computations={%region_7.7_spmd, %region_8.8_spmd} | conditional | flops 1084949120 | bytes 8546324 | solution.py:110
  106.8 2.1 constant_dynamic-slice_fusion.1
  108.9 7.0 %bitcast_add_fusion = f32[128,4,8,128]{3,0,2,1:T(8,128)} fusion(f32[128,4,8,128]{3,0,2,1:T(8,128)} %get-tuple-element.980, bf16[512,4,128,1]{0,2,3,1:T(8,128)(2,1)} %bitcast.159, f32[4,8,128]{2,1,0:T(8,128)S(1)} %get-tuple-element.989, pred[128,512]{0,1:T(8,128)(4,1)S(1)} %compare_and_fusion.1, bf16[512,4,128,1]{0,2,3,1:T(8,128)(2,1)} %bitcast.160, ...), kind=kOutput, calls=%fused_computation.28 | convolution fusion | flops 1084751872 | bytes 6373376 | tf_op jit(solution)/shard_map/while/body/eval_jaxpr/cond/branch_1_fun/kgqs,skd->qkgd/dot_general | solution.py:106
  117.3 3.2 %fusion.41 = f32[128,4,8]{2,1,0:T(4,128)S(1)} fusion(f32[128,4,8,128]{3,0,2,1:T(8,128)} %get-tuple-element.1058, bf16[128,4,8,128]{3,2,1,0:T(8,128)(2,1)} %bitcast.164), kind=kLoop, calls=%fused_computation.66 | loop fusion | flops 1568768 | bytes 3162112 | tf_op jit(solution)/shard_map/reduce_sum | solution.py:124
  125.3 17.2 %while.71 = (s32[]{:T(128)}, f32[128,4,8,128]{3,0,2,1:T(8,128)}, f32[1024,4,128]{2,0,1:T(8,128)}, f32[1024,4,128]{2,0,1:T(8,128)}, s32[]{:T(128)}, /*index=5*/s3...) while((s32[]{:T(128)}, f32[128,4,8,128]{3,0,2,1:T(8,128)}, ...), condition=%wide.region_15.16_spmd.clone, body=%wide.region_12.15_spmd.clone.sunk | while | flops 2712338944 | bytes 89916536 | solution.py:164
  126.6 14.5 %conditional.11 = ((f32[128,4,8,128]{3,0,2,1:T(8,128)}, f32[1024,4,128]{2,0,1:T(8,128)}, f32[1024,4,128]{2,0,1:T(8,128)})) conditional(s32[]{:T(128)} %convert_element_type.91, (f32[128,4,8,128]{3,0,2,1:T(8,128)}, f32[1024,4,128]{2,0,1:T(8,128)}, f32[1024,4,128]{2,0,1:T(8,128)}) %tuple.188, (s32[512]{0:T(512)S(1)}, s32[1,128]{1,0:T(1,128)S(1)}, ...), branch_computations={%region_13.13_spmd, %region_14.14_spmd} | conditional | flops 2712338944 | bytes 89909472 | solution.py:161
  129.3 2.9 fusion.34
  132.2 3.6 %fusion.23 = bf16[4,8,128,512]{2,3,1,0:T(8,128)(2,1)S(1)} fusion(f32[4,512,128,8]{2,1,3,0:T(8,128)S(1)} %fusion.44, f32[4,8,128]{2,1,0:T(8,128)S(1)} %get-tuple-element.1015, f32[4,8,128]{2,1,0:T(8,128)S(1)} %get-tuple-element.1012, pred[128,512]{0,1:T(8,128)(4,1)S(1)} %compare_and_fusion.2, bf16[512,4,128,1]{0,2,3,1:T(8,128)(2,1)S(1)} %bitcast.158, ...), kind=kOutput, calls=%fused_computation.40 | convolution fusion | flops 553648128 | bytes 14254080 | tf_op jit(solution)/shard_map/while/body/eval_jaxpr/cond/branch_1_fun/qkgd,skd->kgqs/dot_general | solution.py:144
  137.3 2.4 bitcast_add_fusion.1
  142.5 3.1 %copy.105 = f32[1024,4,128]{0,2,1:T(8,128)} copy(f32[1024,4,128]{2,0,1:T(8,128)} %get-tuple-element.1061) | data formatting | bytes 4194304 | tf_op jit(solution)/shard_map/while | solution.py:164
  145.6 1.8 copy.104
  148.7 91.4 %while.68 = (s32[]{:T(128)}, f32[128,512]{1,0:T(8,128)S(1)}, f32[128,512]{1,0:T(8,128)S(1)}, s32[]{:T(128)}, f32[1024,512]{0,1:T(8,128)}, /*index=5*/f32[1024,51...) while((s32[]{:T(128)}, f32[128,512]{1,0:T(8,128)S(1)}, f32[128,512]{1,0:T(8,128)S(1)}, s32[]{:T(128)}, ...), condition=%wide.region_17.18_spmd, body=%wide.region_16.17_spmd.sunk | while | flops 262154 | bytes 5767445 | solution.py:188
  152.7 7.2 %collective-permute-done = f32[128,512]{1,0:T(8,128)S(1)} collective-permute-done((f32[128,512]{1,0:T(8,128)S(1)}, f32[128,512]{1,0:T(8,128)S(1)}, u32[]{:S(2)}, u32[]{:S(2)}) %collective-permute-start) | collective-permute-done | bytes 262176 | tf_op jit(solution)/shard_map/while/body/eval_jaxpr/ppermute | solution.py:17
  159.9 3.4 %collective-permute-done.1 = f32[128,512]{1,0:T(8,128)S(1)} collective-permute-done((f32[128,512]{1,0:T(8,128)S(1)}, f32[128,512]{1,0:T(8,128)S(1)}, u32[]{:S(2)}, u32[]{:S(2)}) %collective-permute-start.1) | collective-permute-done | bytes 262176 | tf_op jit(solution)/shard_map/while/body/eval_jaxpr/ppermute | solution.py:17
  167.3 6.9 %collective-permute-done = f32[128,512]{1,0:T(8,128)S(1)} collective-permute-done((f32[128,512]{1,0:T(8,128)S(1)}, f32[128,512]{1,0:T(8,128)S(1)}, u32[]{:S(2)}, u32[]{:S(2)}) %collective-permute-start) | collective-permute-done | bytes 262176 | tf_op jit(solution)/shard_map/while/body/eval_jaxpr/ppermute | solution.py:17
  174.2 2.8 collective-permute-done.1
  181.0 6.3 %collective-permute-done = f32[128,512]{1,0:T(8,128)S(1)} collective-permute-done((f32[128,512]{1,0:T(8,128)S(1)}, f32[128,512]{1,0:T(8,128)S(1)}, u32[]{:S(2)}, u32[]{:S(2)}) %collective-permute-start) | collective-permute-done | bytes 262176 | tf_op jit(solution)/shard_map/while/body/eval_jaxpr/ppermute | solution.py:17
  187.4 2.8 collective-permute-done.1
  194.2 29.8 %collective-permute-done = f32[128,512]{1,0:T(8,128)S(1)} collective-permute-done((f32[128,512]{1,0:T(8,128)S(1)}, f32[128,512]{1,0:T(8,128)S(1)}, u32[]{:S(2)}, u32[]{:S(2)}) %collective-permute-start) | collective-permute-done | bytes 262176 | tf_op jit(solution)/shard_map/while/body/eval_jaxpr/ppermute | solution.py:17
  224.1 2.8 collective-permute-done.1
  230.9 6.5 %collective-permute-done = f32[128,512]{1,0:T(8,128)S(1)} collective-permute-done((f32[128,512]{1,0:T(8,128)S(1)}, f32[128,512]{1,0:T(8,128)S(1)}, u32[]{:S(2)}, u32[]{:S(2)}) %collective-permute-start) | collective-permute-done | bytes 262176 | tf_op jit(solution)/shard_map/while/body/eval_jaxpr/ppermute | solution.py:17
  237.4 2.8 collective-permute-done.1
  240.8 3.3 %all-to-all-start.7 = ((bf16[4,32,512]{2,1,0:T(8,128)(2,1)}), bf16[4,32,512]{2,1,0:T(8,128)(2,1)S(1)}, u32[]{:S(2)}, u32[]{:S(2)}) async-start(bf16[4,32,512]{2,1,0:T(8,128)(2,1)} %bitcast.41), calls=%async_computation.7 | async-start | bytes 262144 | tf_op jit(solution)/shard_map/all_to_all | solution.py:198
  244.9 3.9 %all-to-all-done.7 = bf16[4,32,512]{2,1,0:T(8,128)(2,1)S(1)} async-done(((bf16[4,32,512]{2,1,0:T(8,128)(2,1)}), bf16[4,32,512]{2,1,0:T(8,128)(2,1)S(1)}, u32[]{:S(2)}, u32[]{:S(2)}) %all-to-all-start.7) | async-done | bytes 131104 | tf_op jit(solution)/shard_map/all_to_all | solution.py:198
  248.8 3.3 %all-to-all-start.6 = ((bf16[4,32,512]{2,1,0:T(8,128)(2,1)}), bf16[4,32,512]{2,1,0:T(8,128)(2,1)S(1)}, u32[]{:S(2)}, u32[]{:S(2)}) async-start(bf16[4,32,512]{2,1,0:T(8,128)(2,1)} %bitcast.39), calls=%async_computation.6 | async-start | bytes 262144 | tf_op jit(solution)/shard_map/all_to_all | solution.py:197
  256.7 3.8 %all-to-all-start.3 = ((bf16[4,32,4096]{2,1,0:T(8,128)(2,1)}), bf16[4,32,4096]{2,1,0:T(8,128)(2,1)S(1)}, u32[]{:S(2)}, u32[]{:S(2)}) async-start(bf16[4,32,4096]{2,1,0:T(8,128)(2,1)} %all_to_all.68), calls=%async_computation.3 | async-start | bytes 2097152 | tf_op jit(solution)/shard_map/all_to_all | solution.py:115
  263.9 2.3 all_to_all.73
  266.2 8.5 %all-to-all-done.3 = bf16[4,32,4096]{2,1,0:T(8,128)(2,1)S(1)} async-done(((bf16[4,32,4096]{2,1,0:T(8,128)(2,1)}), bf16[4,32,4096]{2,1,0:T(8,128)(2,1)S(1)}, u32[]{:S(2)}, u32[]{:S(2)}) %all-to-all-start.3) | async-done | bytes 1048608 | tf_op jit(solution)/shard_map/all_to_all | solution.py:115
  274.7 3.5 %all-to-all-start.5 = ((bf16[4,32,4096]{2,1,0:T(8,128)(2,1)}), bf16[4,32,4096]{2,1,0:T(8,128)(2,1)S(1)}, u32[]{:S(2)}, u32[]{:S(2)}) async-start(bf16[4,32,4096]{2,1,0:T(8,128)(2,1)} %all_to_all.73), calls=%async_computation.5 | async-start | bytes 2097152 | tf_op jit(solution)/shard_map/all_to_all | solution.py:190
  282.3 2.2 gather_fusion.3
  284.5 8.1 %all-to-all-done.5 = bf16[4,32,4096]{2,1,0:T(8,128)(2,1)S(1)} async-done(((bf16[4,32,4096]{2,1,0:T(8,128)(2,1)}), bf16[4,32,4096]{2,1,0:T(8,128)(2,1)S(1)}, u32[]{:S(2)}, u32[]{:S(2)}) %all-to-all-start.5) | async-done | bytes 1048608 | tf_op jit(solution)/shard_map/all_to_all | solution.py:190
  292.6 2.2 gather_fusion.5
  (141 shorter events, 59.4 us)
Async XLA Ops:
  7.2 21.5 %copy-start = (bf16[128,4096]{1,0:T(8,128)(2,1)S(1)}, bf16[128,4096]{1,0:T(8,128)(2,1)}, u32[]{:S(2)}) copy-start(bf16[128,4096]{1,0:T(8,128)(2,1)} %param.23) | copy-start | bytes 3145732
  7.2 70.0 %all-gather.3.cloned.1.call-start = ((), (), s32[]{:S(2)}) async-start(), calls=%async_computation.8 | async-start | bytes 1179648 | tf_op jit(solution)/shard_map/all_gather | solution.py:40
  8.0 0.5 copy-start.11
  19.1 82.1 %all-gather.5.cloned.1.call-start = ((), (), s32[]{:S(2)}) async-start(), calls=%async_computation.9 | async-start | bytes 1179648 | tf_op jit(solution)/shard_map/all_gather | solution.py:41
  28.6 5.7 %copy-start.3 = (bf16[128,4096]{1,0:T(8,128)(2,1)S(1)}, bf16[128,4096]{1,0:T(8,128)(2,1)}, u32[]{:S(2)}) copy-start(bf16[128,4096]{1,0:T(8,128)(2,1)} %param.20) | copy-start | bytes 3145732
  30.8 18.0 %all-to-all-start.4 = ((bf16[4,32,4096]{2,1,0:T(8,128)(2,1)}), bf16[4,32,4096]{2,1,0:T(8,128)(2,1)S(1)}, u32[]{:S(2)}, u32[]{:S(2)}) async-start(bf16[4,32,4096]{2,1,0:T(8,128)(2,1)} %bitcast.34), calls=%async_computation.4 | async-start | bytes 2097152 | tf_op jit(solution)/shard_map/all_to_all | solution.py:37
  34.4 18.0 %copy-start.10 = (s32[1,128]{1,0:T(1,128)S(1)}, s32[1,128]{1,0:T(1,128)}, u32[]{:S(2)}) copy-start(s32[1,128]{1,0:T(1,128)} %param.25) | copy-start | bytes 1540
  48.8 24.8 %copy-start.8 = (bf16[4,32,4096]{2,1,0:T(8,128)(2,1)}, bf16[4,32,4096]{2,1,0:T(8,128)(2,1)S(1)}, u32[]{:S(2)}) copy-start(bf16[4,32,4096]{2,1,0:T(8,128)(2,1)S(1)} %all-to-all-done.4) | copy-start | bytes 3145732
  48.8 26.3 %all-to-all-start.1 = ((bf16[4,32,4096]{2,1,0:T(8,128)(2,1)}), bf16[4,32,4096]{2,1,0:T(8,128)(2,1)S(1)}, u32[]{:S(2)}, u32[]{:S(2)}) async-start(bf16[4,32,4096]{2,1,0:T(8,128)(2,1)} %bitcast.30), calls=%async_computation.1 | async-start | bytes 2097152 | tf_op jit(solution)/shard_map/all_to_all | solution.py:34
  75.1 2.1 copy-start.4
  128.0 1.3 copy-start.9
  132.2 3.6 %copy-start.5 = (f32[1024,4,128]{2,0,1:T(8,128)S(1)}, f32[1024,4,128]{2,0,1:T(8,128)}, u32[]{:S(2)}) copy-start(f32[1024,4,128]{2,0,1:T(8,128)} %get-tuple-element.1016) | copy-start | bytes 6291460 | tf_op jit(solution)/shard_map/while/body/eval_jaxpr/cond
  135.7 1.6 copy-start.1
  137.3 2.4 copy-start.6
  139.7 1.4 copy-start.2
  142.5 3.1 %copy-start.7 = (f32[1024,4,128]{2,0,1:T(8,128)S(1)}, f32[1024,4,128]{2,0,1:T(8,128)}, u32[]{:S(2)}) copy-start(f32[1024,4,128]{2,0,1:T(8,128)} %get-tuple-element.1060) | copy-start | bytes 6291460
  148.7 11.1 %collective-permute-start = (f32[128,512]{1,0:T(8,128)S(1)}, f32[128,512]{1,0:T(8,128)S(1)}, u32[]{:S(2)}, u32[]{:S(2)}) collective-permute-start(f32[128,512]{1,0:T(8,128)S(1)} %get-tuple-element.1867), channel_id=1, source_target_pairs={{1,0},{2,1},{3,2},{4,3},{5,4},{6,5},{7,6},{9,8},{10,9},{11,10},{12... | collective-permute-start | bytes 786440 | tf_op jit(solution)/shard_map/while/body/eval_jaxpr/ppermute | solution.py:17
  150.0 13.3 %collective-permute-start.1 = (f32[128,512]{1,0:T(8,128)S(1)}, f32[128,512]{1,0:T(8,128)S(1)}, u32[]{:S(2)}, u32[]{:S(2)}) collective-permute-start(f32[128,512]{1,0:T(8,128)S(1)} %get-tuple-element.1868), channel_id=1, source_target_pairs={{1,0},{2,1},{3,2},{4,3},{5,4},{6,5},{7,6},{9,8},{10,9},{11,10},{12... | collective-permute-start | bytes 786440 | tf_op jit(solution)/shard_map/while/body/eval_jaxpr/ppermute | solution.py:17
  163.4 10.8 %collective-permute-start = (f32[128,512]{1,0:T(8,128)S(1)}, f32[128,512]{1,0:T(8,128)S(1)}, u32[]{:S(2)}, u32[]{:S(2)}) collective-permute-start(f32[128,512]{1,0:T(8,128)S(1)} %get-tuple-element.1867), channel_id=1, source_target_pairs={{1,0},{2,1},{3,2},{4,3},{5,4},{6,5},{7,6},{9,8},{10,9},{11,10},{12... | collective-permute-start | bytes 786440 | tf_op jit(solution)/shard_map/while/body/eval_jaxpr/ppermute | solution.py:17
  164.7 12.3 %collective-permute-start.1 = (f32[128,512]{1,0:T(8,128)S(1)}, f32[128,512]{1,0:T(8,128)S(1)}, u32[]{:S(2)}, u32[]{:S(2)}) collective-permute-start(f32[128,512]{1,0:T(8,128)S(1)} %get-tuple-element.1868), channel_id=1, source_target_pairs={{1,0},{2,1},{3,2},{4,3},{5,4},{6,5},{7,6},{9,8},{10,9},{11,10},{12... | collective-permute-start | bytes 786440 | tf_op jit(solution)/shard_map/while/body/eval_jaxpr/ppermute | solution.py:17
  177.0 10.3 %collective-permute-start = (f32[128,512]{1,0:T(8,128)S(1)}, f32[128,512]{1,0:T(8,128)S(1)}, u32[]{:S(2)}, u32[]{:S(2)}) collective-permute-start(f32[128,512]{1,0:T(8,128)S(1)} %get-tuple-element.1867), channel_id=1, source_target_pairs={{1,0},{2,1},{3,2},{4,3},{5,4},{6,5},{7,6},{9,8},{10,9},{11,10},{12... | collective-permute-start | bytes 786440 | tf_op jit(solution)/shard_map/while/body/eval_jaxpr/ppermute | solution.py:17
  178.3 11.8 %collective-permute-start.1 = (f32[128,512]{1,0:T(8,128)S(1)}, f32[128,512]{1,0:T(8,128)S(1)}, u32[]{:S(2)}, u32[]{:S(2)}) collective-permute-start(f32[128,512]{1,0:T(8,128)S(1)} %get-tuple-element.1868), channel_id=1, source_target_pairs={{1,0},{2,1},{3,2},{4,3},{5,4},{6,5},{7,6},{9,8},{10,9},{11,10},{12... | collective-permute-start | bytes 786440 | tf_op jit(solution)/shard_map/while/body/eval_jaxpr/ppermute | solution.py:17
  190.2 33.8 %collective-permute-start = (f32[128,512]{1,0:T(8,128)S(1)}, f32[128,512]{1,0:T(8,128)S(1)}, u32[]{:S(2)}, u32[]{:S(2)}) collective-permute-start(f32[128,512]{1,0:T(8,128)S(1)} %get-tuple-element.1867), channel_id=1, source_target_pairs={{1,0},{2,1},{3,2},{4,3},{5,4},{6,5},{7,6},{9,8},{10,9},{11,10},{12... | collective-permute-start | bytes 786440 | tf_op jit(solution)/shard_map/while/body/eval_jaxpr/ppermute | solution.py:17
  191.5 35.3 %collective-permute-start.1 = (f32[128,512]{1,0:T(8,128)S(1)}, f32[128,512]{1,0:T(8,128)S(1)}, u32[]{:S(2)}, u32[]{:S(2)}) collective-permute-start(f32[128,512]{1,0:T(8,128)S(1)} %get-tuple-element.1868), channel_id=1, source_target_pairs={{1,0},{2,1},{3,2},{4,3},{5,4},{6,5},{7,6},{9,8},{10,9},{11,10},{12... | collective-permute-start | bytes 786440 | tf_op jit(solution)/shard_map/while/body/eval_jaxpr/ppermute | solution.py:17
  226.9 10.4 %collective-permute-start = (f32[128,512]{1,0:T(8,128)S(1)}, f32[128,512]{1,0:T(8,128)S(1)}, u32[]{:S(2)}, u32[]{:S(2)}) collective-permute-start(f32[128,512]{1,0:T(8,128)S(1)} %get-tuple-element.1867), channel_id=1, source_target_pairs={{1,0},{2,1},{3,2},{4,3},{5,4},{6,5},{7,6},{9,8},{10,9},{11,10},{12... | collective-permute-start | bytes 786440 | tf_op jit(solution)/shard_map/while/body/eval_jaxpr/ppermute | solution.py:17
  228.2 11.9 %collective-permute-start.1 = (f32[128,512]{1,0:T(8,128)S(1)}, f32[128,512]{1,0:T(8,128)S(1)}, u32[]{:S(2)}, u32[]{:S(2)}) collective-permute-start(f32[128,512]{1,0:T(8,128)S(1)} %get-tuple-element.1868), channel_id=1, source_target_pairs={{1,0},{2,1},{3,2},{4,3},{5,4},{6,5},{7,6},{9,8},{10,9},{11,10},{12... | collective-permute-start | bytes 786440 | tf_op jit(solution)/shard_map/while/body/eval_jaxpr/ppermute | solution.py:17
  240.8 7.9 %all-to-all-start.7 = ((bf16[4,32,512]{2,1,0:T(8,128)(2,1)}), bf16[4,32,512]{2,1,0:T(8,128)(2,1)S(1)}, u32[]{:S(2)}, u32[]{:S(2)}) async-start(bf16[4,32,512]{2,1,0:T(8,128)(2,1)} %bitcast.41), calls=%async_computation.7 | async-start | bytes 262144 | tf_op jit(solution)/shard_map/all_to_all | solution.py:198
  248.8 7.9 %all-to-all-start.6 = ((bf16[4,32,512]{2,1,0:T(8,128)(2,1)}), bf16[4,32,512]{2,1,0:T(8,128)(2,1)S(1)}, u32[]{:S(2)}, u32[]{:S(2)}) async-start(bf16[4,32,512]{2,1,0:T(8,128)(2,1)} %bitcast.39), calls=%async_computation.6 | async-start | bytes 262144 | tf_op jit(solution)/shard_map/all_to_all | solution.py:197
  256.7 18.0 %all-to-all-start.3 = ((bf16[4,32,4096]{2,1,0:T(8,128)(2,1)}), bf16[4,32,4096]{2,1,0:T(8,128)(2,1)S(1)}, u32[]{:S(2)}, u32[]{:S(2)}) async-start(bf16[4,32,4096]{2,1,0:T(8,128)(2,1)} %all_to_all.68), calls=%async_computation.3 | async-start | bytes 2097152 | tf_op jit(solution)/shard_map/all_to_all | solution.py:115
  274.7 18.0 %all-to-all-start.5 = ((bf16[4,32,4096]{2,1,0:T(8,128)(2,1)}), bf16[4,32,4096]{2,1,0:T(8,128)(2,1)S(1)}, u32[]{:S(2)}, u32[]{:S(2)}) async-start(bf16[4,32,4096]{2,1,0:T(8,128)(2,1)} %all_to_all.73), calls=%async_computation.5 | async-start | bytes 2097152 | tf_op jit(solution)/shard_map/all_to_all | solution.py:190
Sparse Core Ops, SparseCore 0:
  19.2 40.8 all-gather.2
  62.2 38.9 all-gather.4
where the time goes:
time: 304 us; the launch traced here: 302 us
  waiting for transfers between devices  120 us (39%)
  local copies, waits for them, and re-layouts  57.5 us (19%)
  blocking collectives  37.7 us (12%)
  starting transfers between devices  34 us (11%)
  matrix products  19.8 us (7%)
  between operations  14.4 us (5%)
  other arithmetic  13 us (4%)
  loops' own time  4.74 us (2%)
    ppermute x10, waiting for transfers between devices, passed_along(): lax.ppermute(value, axis, [(source, source + steps) for source in range(f...  71.1 us
    all_gather x1, blocking collectives, on_device(): lax.all_gather(segments, 'ctx', axis=1, tiled=True)  21.3 us
    all_gather x1, waiting for transfers between devices, on_device(): lax.all_gather(v_rows, 'ctx', axis=0, tiled=True)  15.7 us
    ppermute x10, starting transfers between devices, passed_along(): lax.ppermute(value, axis, [(source, source + steps) for source in range(f...  12.9 us
    all_to_all x1, waiting for transfers between devices, on_device(): lax.all_to_all(out_grad[row_plan], 'dp', split_axis=0, concat_axis=0, til...  12.2 us
    all_to_all x1, blocking collectives, on_device(): lax.all_to_all(key_proj[row_plan], 'dp', split_axis=0, concat_axis=0, til...  8.75 us
    all_to_all x1, waiting for transfers between devices, on_device(): lax.all_to_all(out.astype(jnp.bfloat16).reshape(rows_here, -1), 'dp', spl...  8.46 us
    all_to_all x1, waiting for transfers between devices, on_device(): lax.all_to_all(q_grad.astype(jnp.bfloat16).reshape(rows_here, -1), 'dp',...  8.12 us
  transfers between devices with their start and end apart: 18, of which 16 were waited for; matrix products, arithmetic and copies ran while one was open for 12% of the time, Pallas kernels for 0%

commit v1 on v0

v1 whole, which is shorter than its diff:
```python
import functools
import math

import jax
import jax.numpy as jnp
from jax import lax
from jax.experimental import pallas as pl
from jax.experimental.pallas import tpu as pltpu
from jax.sharding import PartitionSpec as P

HEADS = 32
KV_HEADS = 4
HEAD_DIM = 128
GROUP = HEADS // KV_HEADS
WIDE = GROUP * HEAD_DIM

NEG = -1e30
MESH = pl.DeviceIdType.MESH
F32 = jnp.float32
BF16 = jnp.bfloat16


def dot(lhs, rhs):
    return jnp.dot(lhs, rhs, preferred_element_type=F32)


def dot_nt(lhs, rhs):
    return lax.dot_general(lhs, rhs, (((1,), (1,)), ((), ())), preferred_element_type=F32)


def kernel(
    n_dp, n_ctx, reach,
    q_ref, k_ref, v_ref, d_ref, plan_ref, seg_ref,
    att_ref, qg_ref, kg_ref, vg_ref,
    kv_out, qd_out, kv, qd, segs, res, back, own, term_out, term_in, sum_out, sum_back,
    bias, q_cat, d_cat, w_t, ds_t,
    kv_s, kv_r, qd_s, qd_r, ctx_s, ctx_r, seg_s, seg_r, res_s, res_r, term_s, term_r, sum_s, sum_r,
):
    rows = q_ref.shape[0]
    share = rows // n_dp
    keys = (reach + 1) * rows
    scaling = HEAD_DIM ** (-0.5)
    a = lax.axis_index("dp")
    c = lax.axis_index("ctx")

    barrier = pltpu.get_barrier_semaphore()
    for i in range(1, n_dp):
        pl.semaphore_signal(
            barrier, inc=1, device_id={"dp": lax.rem(a + i, n_dp)}, device_id_type=MESH
        )
    for i in range(1, n_ctx):
        pl.semaphore_signal(
            barrier, inc=1, device_id={"ctx": lax.rem(c + i, n_ctx)}, device_id_type=MESH
        )

    def to_dp(src, dst, i, g, send, recv):
        peer = lax.rem(a + i, n_dp)
        return pltpu.make_async_remote_copy(
            src_ref=src.at[g, peer],
            dst_ref=dst(g),
            send_sem=send.at[g, i - 1],
            recv_sem=recv.at[g, i - 1],
            device_id={"dp": peer},
            device_id_type=MESH,
        )

    def kv_copy(g, i):
        return to_dp(kv_out, lambda g: kv.at[g, 0, a], i, g, kv_s, kv_r)

    def qd_copy(g, i):
        return to_dp(qd_out, lambda g: qd.at[g, a], i, g, qd_s, qd_r)

    def res_copy(g, i):
        return to_dp(res, lambda g: back.at[g, a], i, g, res_s, res_r)

    def sum_copy(g, i):
        return to_dp(sum_out, lambda g: sum_back.at[g, a], i, g, sum_s, sum_r)

    def ctx_copy(g, r):
        return pltpu.make_async_remote_copy(
            src_ref=kv.at[g, 0],
            dst_ref=kv.at[g, r],
            send_sem=ctx_s.at[g, r - 1],
            recv_sem=ctx_r.at[g, r - 1],
            device_id={"ctx": lax.rem(c + r, n_ctx)},
            device_id_type=MESH,
        )

    def seg_copy(r):
        return pltpu.make_async_remote_copy(
            src_ref=segs.at[0],
            dst_ref=segs.at[r],
            send_sem=seg_s.at[r - 1],
            recv_sem=seg_r.at[r - 1],
            device_id={"ctx": lax.rem(c + r, n_ctx)},
            device_id_type=MESH,
        )

    def term_copy(g, r):
        return pltpu.make_async_remote_copy(
            src_ref=term_out.at[g, r - 1],
            dst_ref=term_in.at[g, r - 1],
            send_sem=term_s.at[g, r - 1],
            recv_sem=term_r.at[g, r - 1],
            device_id={"ctx": lax.rem(c + n_ctx - r, n_ctx)},
            device_id_type=MESH,
        )

    heads = range(KV_HEADS)
    peers = range(1, n_dp)
    hops = range(1, reach + 1)

    def has_higher(r):
        return pl.when(c + r < n_ctx)

    def has_lower(r):
        return pl.when(c >= r)

    plan_row = jnp.broadcast_to(plan_ref[...], (rows, rows))
    unpack_f = jnp.where(
        lax.broadcasted_iota(jnp.int32, (rows, rows), 0) == plan_row, 1.0, 0.0
    ).astype(F32)
    unpack = unpack_f.astype(BF16)
    pack = unpack_f.T.astype(BF16)

    def packed(value):
        return dot(pack, value).astype(BF16).reshape(n_dp, share, value.shape[1])

    for g in heads:
        cols = slice(g * HEAD_DIM, (g + 1) * HEAD_DIM)
        kv_out[g, :, :, :HEAD_DIM] = packed(k_ref[:, cols])
        kv_out[g, :, :, HEAD_DIM:] = packed(v_ref[:, cols])
    segs[0] = jnp.broadcast_to(seg_ref[...], (8, rows))

    pl.semaphore_wait(barrier, n_dp - 1 + n_ctx - 1)

    for g in heads:
        for i in peers:
            kv_copy(g, i).start()
        kv[g, 0, a] = kv_out[g, a]
    for r in hops:

        @has_higher(r)
        def _():
            seg_copy(r).start()

    for g in heads:
        cols = slice(g * WIDE, (g + 1) * WIDE)
        qd_out[g, :, :, :WIDE] = packed(q_ref[:, cols])
        qd_out[g, :, :, WIDE:] = packed(d_ref[:, cols])
        for i in peers:
            qd_copy(g, i).start()
        qd[g, a] = qd_out[g, a]

    for g in heads:
        for i in peers:
            kv_copy(g, i).wait_recv()
        for r in hops:

            @has_higher(r)
            def _():
                ctx_copy(g, r).start()

    for r in hops:

        @pl.when(c < r)
        def _():
            segs[r] = jnp.full((8, rows), -1, jnp.int32)
            for g in heads:
                kv[g, r] = jnp.zeros(kv.shape[2:], BF16)

        @pl.when(c + r >= n_ctx)
        def _():
            for g in heads:
                term_in[g, r - 1] = jnp.zeros(term_in.shape[2:], BF16)

    for r in hops:

        @has_lower(r)
        def _():
            seg_copy(r).wait_recv()

    row_seg = jnp.broadcast_to(seg_ref[...], (rows, rows)).astype(F32)
    for r in range(reach + 1):
        key_seg = jnp.broadcast_to(segs[r, 0:1, :], (rows, rows)).astype(F32).T
        visible = key_seg == row_seg
        if r == 0:
            visible = visible & (
                lax.broadcasted_iota(jnp.int32, (rows, rows), 0)
                <= lax.broadcasted_iota(jnp.int32, (rows, rows), 1)
            )
        masked = jnp.where(visible, 0.0, NEG).astype(F32)
        bias[r * rows : (r + 1) * rows, :rows] = masked
        bias[r * rows : (r + 1) * rows, rows:] = masked

    def attend(g):
        k_blk = kv[g, :, :, :, :HEAD_DIM].reshape(keys, HEAD_DIM)
        v_blk = kv[g, :, :, :, HEAD_DIM:].reshape(keys, HEAD_DIM)
        for h in range(GROUP):
            into = slice(h * rows, (h + 1) * rows)
            cols = slice(h * HEAD_DIM, (h + 1) * HEAD_DIM)
            d_cols = slice(WIDE + h * HEAD_DIM, WIDE + (h + 1) * HEAD_DIM)
            q_cat[into, :] = qd[g, :, :, cols].reshape(rows, HEAD_DIM)
            d_cat[into, :] = qd[g, :, :, d_cols].reshape(rows, HEAD_DIM)

        def pair(step, carry):
            at = pl.multiple_of(step * (2 * rows), 2 * rows)
            span = pl.ds(at, 2 * rows)
            scores = dot_nt(k_blk, q_cat[span, :]) * (scaling * math.log2(math.e)) + bias[...]
            dprobs = dot_nt(v_blk, d_cat[span, :])
            top = jnp.max(scores, axis=0, keepdims=True)
            expd = jnp.exp2(scores - top)
            probs = expd * (1.0 / jnp.sum(expd, axis=0, keepdims=True))
            weights = probs.astype(BF16)
            w_t[:, span] = weights
            row_dot = jnp.sum(weights.astype(F32) * dprobs, axis=0, keepdims=True)
            ds_t[:, span] = (probs * (dprobs - row_dot) * scaling).astype(BF16)
            return carry

        lax.fori_loop(0, GROUP // 2, pair, 0)
        k_term = dot(ds_t[...], q_cat[...])
        v_term = dot(w_t[...], d_cat[...])
        own[g, :, :HEAD_DIM] = k_term[:rows]
        own[g, :, HEAD_DIM:] = v_term[:rows]
        for r in hops:
            part = slice(r * rows, (r + 1) * rows)
            term_out[g, r - 1, :, :HEAD_DIM] = k_term[part].astype(BF16)
            term_out[g, r - 1, :, HEAD_DIM:] = v_term[part].astype(BF16)
        for r in hops:

            @has_lower(r)
            def _():
                term_copy(g, r).start()

        v_t = v_blk.astype(F32).T.astype(BF16)
        k_t = k_blk.astype(F32).T.astype(BF16)
        out_t = dot(v_t, w_t[...])
        dq_t = dot(k_t, ds_t[...])
        for h in range(GROUP):
            part = slice(h * rows, (h + 1) * rows)
            cols = slice(h * HEAD_DIM, (h + 1) * HEAD_DIM)
            d_cols = slice(WIDE + h * HEAD_DIM, WIDE + (h + 1) * HEAD_DIM)
            res[g, :, :, cols] = out_t[:, part].T.astype(BF16).reshape(n_dp, share, HEAD_DIM)
            res[g, :, :, d_cols] = dq_t[:, part].T.astype(BF16).reshape(n_dp, share, HEAD_DIM)
        for i in peers:
            res_copy(g, i).start()
        back[g, a] = res[g, a]

    def finish_terms(g):
        total = own[g]
        for r in hops:

            @has_higher(r)
            def _():
                term_copy(g, r).wait_recv()

        for r in hops:
            total = total + term_in[g, r - 1].astype(F32)
        sum_out[g] = total.astype(BF16).reshape(n_dp, share, 2 * HEAD_DIM)
        for i in peers:
            sum_copy(g, i).start()
        sum_back[g, a] = sum_out[g, a]

    def finish_rows(g):
        for i in peers:
            res_copy(g, i).wait_recv()
        cols = slice(g * WIDE, (g + 1) * WIDE)
        got = back[g].reshape(rows, 2 * WIDE)
        att_ref[:, cols] = dot(unpack, got[:, :WIDE]).astype(BF16)
        qg_ref[:, cols] = dot(unpack, got[:, WIDE:]).astype(BF16)

    def finish_sums(g):
        for i in peers:
            sum_copy(g, i).wait_recv()
        cols = slice(g * HEAD_DIM, (g + 1) * HEAD_DIM)
        got = dot(unpack, sum_back[g].reshape(rows, 2 * HEAD_DIM)).astype(BF16)
        kg_ref[:, cols] = got[:, :HEAD_DIM]
        vg_ref[:, cols] = got[:, HEAD_DIM:]

    for g in heads:
        for i in peers:
            qd_copy(g, i).wait_recv()
        for r in hops:

            @has_lower(r)
            def _():
                ctx_copy(g, r).wait_recv()

        attend(g)
        if g >= 1:
            finish_terms(g - 1)
        if g >= 2:
            finish_rows(g - 2)
    last = KV_HEADS - 1
    finish_rows(last - 1)
    finish_terms(last)
    finish_rows(last)
    for g in heads:
        finish_sums(g)

    for g in heads:
        for i in peers:
            kv_copy(g, i).wait_send()
            qd_copy(g, i).wait_send()
            res_copy(g, i).wait_send()
            sum_copy(g, i).wait_send()
    for r in hops:

        @has_higher(r)
        def _():
            seg_copy(r).wait_send()
            for g in heads:
                ctx_copy(g, r).wait_send()

        @has_lower(r)
        def _():
            for g in heads:
                term_copy(g, r).wait_send()


def on_device(queries, key_proj, value_proj, out_grad, row_plan, segments):
    n_dp = lax.axis_size("dp")
    n_ctx = lax.axis_size("ctx")
    rows = queries.shape[0]
    share = rows // n_dp
    reach = min(n_ctx // 2 + 1, n_ctx - 1)
    keys = (reach + 1) * rows
    stacked = GROUP * rows
    vmem = pl.BlockSpec(memory_space=pltpu.VMEM)
    dma = pltpu.SemaphoreType.DMA
    dp_sem = dma((KV_HEADS, n_dp - 1))
    hop_sem = dma((KV_HEADS, reach))
    narrow = (n_dp, share, 2 * HEAD_DIM)
    broad = (KV_HEADS, n_dp, share, 2 * WIDE)
    scratch = [
        pltpu.VMEM((KV_HEADS, *narrow), BF16),
        pltpu.VMEM(broad, BF16),
        pltpu.VMEM((KV_HEADS, reach + 1, *narrow), BF16),
        pltpu.VMEM(broad, BF16),
        pltpu.VMEM((reach + 1, 8, rows), jnp.int32),
        pltpu.VMEM(broad, BF16),
        pltpu.VMEM(broad, BF16),
        pltpu.VMEM((KV_HEADS, rows, 2 * HEAD_DIM), F32),
        pltpu.VMEM((KV_HEADS, reach, rows, 2 * HEAD_DIM), BF16),
        pltpu.VMEM((KV_HEADS, reach, rows, 2 * HEAD_DIM), BF16),
        pltpu.VMEM((KV_HEADS, *narrow), BF16),
        pltpu.VMEM((KV_HEADS, *narrow), BF16),
        pltpu.VMEM((keys, 2 * rows), F32),
        pltpu.VMEM((stacked, HEAD_DIM), BF16),
        pltpu.VMEM((stacked, HEAD_DIM), BF16),
        pltpu.VMEM((keys, stacked), BF16),
        pltpu.VMEM((keys, stacked), BF16),
        dp_sem, dp_sem,
        dp_sem, dp_sem,
        hop_sem, hop_sem,
        dma((reach,)), dma((reach,)),
        dp_sem, dp_sem,
        hop_sem, hop_sem,
        dp_sem, dp_sem,
    ]
    return pl.pallas_call(
        functools.partial(kernel, n_dp, n_ctx, reach),
        out_shape=(
            jax.ShapeDtypeStruct(queries.shape, BF16),
            jax.ShapeDtypeStruct(queries.shape, BF16),
            jax.ShapeDtypeStruct(key_proj.shape, BF16),
            jax.ShapeDtypeStruct(value_proj.shape, BF16),
        ),
        in_specs=[vmem] * 6,
        out_specs=(vmem,) * 4,
        scratch_shapes=scratch,
        compiler_params=pltpu.CompilerParams(
            collective_id=0, has_side_effects=True, vmem_limit_bytes=56 * 1024 * 1024
        ),
        cost_estimate=pl.CostEstimate(
            flops=12 * HEADS * rows * keys * HEAD_DIM,
            bytes_accessed=4 * queries.size * 2,
            transcendentals=HEADS * rows * keys,
        ),
    )(queries, key_proj, value_proj, out_grad, row_plan.reshape(1, rows), segments)


def solution(mesh):
    placed = (
        P(("dp", "ctx"), None),
        P(("dp", "ctx"), None),
        P(("dp", "ctx"), None),
        P(("dp", "ctx"), None),
        P(("dp", "ctx")),
        P("dp", "ctx"),
    )
    return jax.shard_map(
        on_device,
        mesh=mesh,
        in_specs=placed,
        out_specs=(
            P(("dp", "ctx"), None),
            P(("dp", "ctx"), None),
            P(("dp", "ctx"), None),
            P(("dp", "ctx"), None),
        ),
        check_vma=False,
    )
```

time: 304 us -> 81 us (0.27)
  waiting for transfers between devices: 120 us -> 0 us
  Pallas kernels: 0 us -> 75.2 us
  local copies, waits for them, and re-layouts: 57.5 us -> 5.01 us
  blocking collectives: 37.7 us -> 0 us
  starting transfers between devices: 34 us -> 0 us
  matrix products: 19.8 us -> 0 us
  between operations: 14.4 us -> 0.65 us
  other arithmetic: 13 us -> 0 us
  loops' own time: 4.74 us -> 0 us
    pallas_call x0 -> x1, Pallas kernels: none -> 75.2 us  [on_device(): pl.pallas_call(functools.partial(kernel, n_dp, n_ctx, reach), out_shape=(...]
    ppermute x10 -> x0, waiting for transfers between devices: 71.1 us -> none  [passed_along(): lax.ppermute(value, axis, [(source, source + steps) for source in range(f...]
    all_to_all x6 -> x0, waiting for transfers between devices: 33.6 us -> none  [the longest x1 12.2 us: on_device(): lax.all_to_all(out_grad[row_plan], 'dp', split_axis=0, concat_axis=0, til...]
    all_gather x1 -> x0, blocking collectives: 21.3 us -> none  [on_device(): lax.all_gather(segments, 'ctx', axis=1, tiled=True)]
    all_to_all x6 -> x0, starting transfers between devices: 21 us -> none  [the longest x1 3.78 us: on_device(): lax.all_to_all(out.astype(jnp.bfloat16).reshape(rows_here, -1), 'dp', spl...]
    dot_general x7 -> x0, matrix products: 19.8 us -> none  [the longest x1 7 us: output_compute(): jnp.einsum('kgqs,skd->qkgd', weights, val_blk, preferred_element_type=jnp...]
    all_to_all x2 -> x0, blocking collectives: 16.4 us -> none  [the longest x1 8.75 us: on_device(): lax.all_to_all(key_proj[row_plan], 'dp', split_axis=0, concat_axis=0, til...]
    all_gather x2 -> x0, waiting for transfers between devices: 15.7 us -> none  [the longest x1 15.7 us: on_device(): lax.all_gather(v_rows, 'ctx', axis=0, tiled=True)]
  transfers between devices with their start and end apart: 18 -> 0, of which waited for: 16 -> 0; matrix products, arithmetic and copies ran while one was open for 12% -> 0% of each run, Pallas kernels for 0% -> 0%
where the time goes in v1:
time: 81 us; the launch traced here: 80.8 us
  Pallas kernels  75.2 us (93%)
  local copies, waits for them, and re-layouts  5.01 us (6%)
    pallas_call x1, Pallas kernels, on_device(): pl.pallas_call(functools.partial(kernel, n_dp, n_ctx, reach), out_shape=(...  75.2 us
    unnamed x10, local copies, waits for them, and re-layouts  5.01 us

profile of v1, /device:TPU:0, one launch (start us, length us, event | category | flops | bytes accessed | tf_op | source)
XLA Modules:
  0.0 80.8 jit_solution(719503112712226072)
XLA Ops:
  0.6 75.2 %shard_map.93 = (bf16[128,4096]{1,0:T(8,128)(2,1)}, bf16[128,4096]{1,0:T(8,128)(2,1)}, bf16[128,512]{1,0:T(8,128)(2,1)}, bf16[128,512]{1,0:T(8,128)(2,1)}) custom-call(bf16[128,4096]{1,0:T(8,128)(2,1)} %q_ref.1, bf16[128,512]{1,0:T(8,128)(2,1)} %k_ref.1, bf16[128,512]{1,0:T(8,128)(2,1)} %v_ref.1, bf16[128,4096]{1,0:T(8,128)(2,1)} %d_ref.1, ...), custom_call_target="tpu_custom_call" | custom-call | flops 4831838208 | bytes 4194304 | tf_op jit(solution)/shard_map/pallas_call | solution.py:361
  75.8 0.0 copy-start
  75.8 2.4 %copy.14 = bf16[128,4096]{1,0:T(8,128)(2,1)} copy(bf16[128,4096]{1,0:T(8,128)(2,1)} %get-tuple-element.8) | data formatting | bytes 2097152
  78.2 0.0 copy-done
  78.2 0.0 copy-start.2
  78.2 1.0 %copy.15 = bf16[128,4096]{1,0:T(8,128)(2,1)} copy(bf16[128,4096]{1,0:T(8,128)(2,1)S(1)} %copy-done) | data formatting | bytes 2097152
  79.2 0.1 copy-done.2
  79.2 0.0 copy-start.1
  79.2 0.7 copy.16
  79.9 0.3 copy-done.1
  80.2 0.7 copy.17
Async XLA Ops:
  75.8 2.4 %copy-start = (bf16[128,4096]{1,0:T(8,128)(2,1)S(1)}, bf16[128,4096]{1,0:T(8,128)(2,1)}, u32[]{:S(2)}) copy-start(bf16[128,4096]{1,0:T(8,128)(2,1)} %get-tuple-element.9) | copy-start | bytes 3145732
  78.2 1.0 %copy-start.2 = (bf16[128,512]{1,0:T(8,128)(2,1)S(1)}, bf16[128,512]{1,0:T(8,128)(2,1)}, u32[]{:S(2)}) copy-start(bf16[128,512]{1,0:T(8,128)(2,1)} %get-tuple-element.10) | copy-start | bytes 393220
  79.2 1.0 %copy-start.1 = (bf16[128,512]{1,0:T(8,128)(2,1)S(1)}, bf16[128,512]{1,0:T(8,128)(2,1)}, u32[]{:S(2)}) copy-start(bf16[128,512]{1,0:T(8,128)(2,1)} %get-tuple-element.11) | copy-start | bytes 393220

commit v2 on v1

--- a/solution.py
+++ b/solution.py
@@ -28,13 +28,31 @@
     return lax.dot_general(lhs, rhs, (((1,), (1,)), ((), ())), preferred_element_type=F32)
 
 
+def unpacking(plan_ref):
+    rows = plan_ref.shape[1]
+    plan_row = jnp.broadcast_to(plan_ref[...], (rows, rows))
+    here = lax.broadcasted_iota(jnp.int32, (rows, rows), 0) == plan_row
+    return jnp.where(here, 1.0, 0.0).astype(F32)
+
+
+def unpack_kernel(plan_ref, back_ref, sums_ref, att_ref, qg_ref, kg_ref, vg_ref):
+    rows = plan_ref.shape[1]
+    unpack = unpacking(plan_ref).astype(BF16)
+    got = back_ref[0].reshape(rows, 2 * WIDE)
+    att_ref[...] = dot(unpack, got[:, :WIDE]).astype(BF16)
+    qg_ref[...] = dot(unpack, got[:, WIDE:]).astype(BF16)
+    sums = dot(unpack, sums_ref[0].reshape(rows, 2 * HEAD_DIM)).astype(BF16)
+    kg_ref[...] = sums[:, :HEAD_DIM]
+    vg_ref[...] = sums[:, HEAD_DIM:]
+
+
 def kernel(
     n_dp, n_ctx, reach,
     q_ref, k_ref, v_ref, d_ref, plan_ref, seg_ref,
-    att_ref, qg_ref, kg_ref, vg_ref,
-    kv_out, qd_out, kv, qd, segs, res, back, own, term_out, term_in, sum_out, sum_back,
+    back, sum_back,
+    kv_out, qd_out, kv, qd, segs, res, own, term_out, term_in, sum_out,
     bias, q_cat, d_cat, w_t, ds_t,
-    kv_s, kv_r, qd_s, qd_r, ctx_s, ctx_r, seg_s, seg_r, res_s, res_r, term_s, term_r, sum_s, sum_r,
+    kv_s, kv_r, qd_s, qd_r, ctx_s, ctx_r, beside_s, seg_s, seg_r, res_s, res_r, term_s, term_r, sum_s, sum_r,
 ):
     rows = q_ref.shape[0]
     share = rows // n_dp
@@ -86,6 +104,34 @@
             device_id_type=MESH,
         )
 
+    def beside_copy(g, r):
+        low = lax.rem(c, 2) == 0
+        there = jnp.where(low, r + 1, r - 1) if r else r + 1
+        return pltpu.make_async_remote_copy(
+            src_ref=kv.at[g, r],
+            dst_ref=kv.at[g, there],
+            send_sem=beside_s.at[g, r // 2],
+            recv_sem=ctx_r.at[g, there - 1],
+            device_id={"ctx": jnp.where(low, c + 1, c - 1)},
+            device_id_type=MESH,
+        )
+
+    def beside(r):
+        low = lax.rem(c, 2) == 0
+        if r == 0:
+            return pl.when(low)
+        if r + 1 <= reach:
+            return pl.when(c >= r)
+        return pl.when((c >= r) & jnp.logical_not(low))
+
+    def far(r):
+        if r % 2 == 0:
+            return pl.when(c + r < n_ctx)
+        return pl.when((c + r < n_ctx) & (lax.rem(c, 2) == 1))
+
+    straight = [r for r in range(1, reach + 1) if r % 2 == 0 or r == reach]
+    passed = range(0, reach + 1, 2)
+
     def seg_copy(r):
         return pltpu.make_async_remote_copy(
             src_ref=segs.at[0],
@@ -116,12 +162,7 @@
     def has_lower(r):
         return pl.when(c >= r)
 
-    plan_row = jnp.broadcast_to(plan_ref[...], (rows, rows))
-    unpack_f = jnp.where(
-        lax.broadcasted_iota(jnp.int32, (rows, rows), 0) == plan_row, 1.0, 0.0
-    ).astype(F32)
-    unpack = unpack_f.astype(BF16)
-    pack = unpack_f.T.astype(BF16)
+    pack = unpacking(plan_ref).T.astype(BF16)
 
     def packed(value):
         return dot(pack, value).astype(BF16).reshape(n_dp, share, value.shape[1])
@@ -155,11 +196,15 @@
     for g in heads:
         for i in peers:
             kv_copy(g, i).wait_recv()
-        for r in hops:
-
-            @has_higher(r)
+        for r in straight:
+
+            @far(r)
             def _():
                 ctx_copy(g, r).start()
+
+        @beside(0)
+        def _():
+            beside_copy(g, 0).start()
 
     for r in hops:
 
@@ -261,26 +306,24 @@
             sum_copy(g, i).start()
         sum_back[g, a] = sum_out[g, a]
 
-    def finish_rows(g):
-        for i in peers:
-            res_copy(g, i).wait_recv()
-        cols = slice(g * WIDE, (g + 1) * WIDE)
-        got = back[g].reshape(rows, 2 * WIDE)
-        att_ref[:, cols] = dot(unpack, got[:, :WIDE]).astype(BF16)
-        qg_ref[:, cols] = dot(unpack, got[:, WIDE:]).astype(BF16)
-
-    def finish_sums(g):
-        for i in peers:
-            sum_copy(g, i).wait_recv()
-        cols = slice(g * HEAD_DIM, (g + 1) * HEAD_DIM)
-        got = dot(unpack, sum_back[g].reshape(rows, 2 * HEAD_DIM)).astype(BF16)
-        kg_ref[:, cols] = got[:, :HEAD_DIM]
-        vg_ref[:, cols] = got[:, HEAD_DIM:]
-
-    for g in heads:
+    def pass_on(g):
+        for r in passed[1:]:
+
+            @has_lower(r)
+            def _():
+                ctx_copy(g, r).wait_recv()
+
+            @beside(r)
+            def _():
+                beside_copy(g, r).start()
+
+    pass_on(0)
+    for g in heads:
+        if g + 1 < KV_HEADS:
+            pass_on(g + 1)
         for i in peers:
             qd_copy(g, i).wait_recv()
-        for r in hops:
+        for r in hops[::2]:
 
             @has_lower(r)
             def _():
@@ -289,14 +332,11 @@
         attend(g)
         if g >= 1:
             finish_terms(g - 1)
-        if g >= 2:
-            finish_rows(g - 2)
-    last = KV_HEADS - 1
-    finish_rows(last - 1)
-    finish_terms(last)
-    finish_rows(last)
-    for g in heads:
-        finish_sums(g)
+    finish_terms(KV_HEADS - 1)
+    for g in heads:
+        for i in peers:
+            res_copy(g, i).wait_recv()
+            sum_copy(g, i).wait_recv()
 
     for g in heads:
         for i in peers:
@@ -309,13 +349,25 @@
         @has_higher(r)
         def _():
             seg_copy(r).wait_send()
+
+        @has_lower(r)
+        def _():
+            for g in heads:
+                term_copy(g, r).wait_send()
+
+    for r in straight:
+
+        @far(r)
+        def _():
             for g in heads:
                 ctx_copy(g, r).wait_send()
 
-        @has_lower(r)
+    for r in passed:
+
+        @beside(r)
         def _():
             for g in heads:
-                term_copy(g, r).wait_send()
+                beside_copy(g, r).wait_send()
 
 
 def on_device(queries, key_proj, value_proj, out_grad, row_plan, segments):
@@ -339,11 +391,9 @@
         pltpu.VMEM(broad, BF16),
         pltpu.VMEM((reach + 1, 8, rows), jnp.int32),
         pltpu.VMEM(broad, BF16),
-        pltpu.VMEM(broad, BF16),
         pltpu.VMEM((KV_HEADS, rows, 2 * HEAD_DIM), F32),
         pltpu.VMEM((KV_HEADS, reach, rows, 2 * HEAD_DIM), BF16),
         pltpu.VMEM((KV_HEADS, reach, rows, 2 * HEAD_DIM), BF16),
-        pltpu.VMEM((KV_HEADS, *narrow), BF16),
         pltpu.VMEM((KV_HEADS, *narrow), BF16),
         pltpu.VMEM((keys, 2 * rows), F32),
         pltpu.VMEM((stacked, HEAD_DIM), BF16),
@@ -353,21 +403,21 @@
         dp_sem, dp_sem,
         dp_sem, dp_sem,
         hop_sem, hop_sem,
+        dma((KV_HEADS, reach // 2 + 1)),
         dma((reach,)), dma((reach,)),
         dp_sem, dp_sem,
         hop_sem, hop_sem,
         dp_sem, dp_sem,
     ]
-    return pl.pallas_call(
+    plan = row_plan.reshape(1, rows)
+    back, sums = pl.pallas_call(
         functools.partial(kernel, n_dp, n_ctx, reach),
         out_shape=(
-            jax.ShapeDtypeStruct(queries.shape, BF16),
-            jax.ShapeDtypeStruct(queries.shape, BF16),
-            jax.ShapeDtypeStruct(key_proj.shape, BF16),
-            jax.ShapeDtypeStruct(value_proj.shape, BF16),
+            jax.ShapeDtypeStruct(broad, BF16),
+            jax.ShapeDtypeStruct((KV_HEADS, *narrow), BF16),
         ),
         in_specs=[vmem] * 6,
-        out_specs=(vmem,) * 4,
+        out_specs=(vmem,) * 2,
         scratch_shapes=scratch,
         compiler_params=pltpu.CompilerParams(
             collective_id=0, has_side_effects=True, vmem_limit_bytes=56 * 1024 * 1024
@@ -377,7 +427,25 @@
             bytes_accessed=4 * queries.size * 2,
             transcendentals=HEADS * rows * keys,
         ),
-    )(queries, key_proj, value_proj, out_grad, row_plan.reshape(1, rows), segments)
+    )(queries, key_proj, value_proj, out_grad, plan, segments)
+    wide_block = pl.BlockSpec((rows, WIDE), lambda g: (0, g))
+    head_block = pl.BlockSpec((rows, HEAD_DIM), lambda g: (0, g))
+    return pl.pallas_call(
+        unpack_kernel,
+        grid=(KV_HEADS,),
+        out_shape=(
+            jax.ShapeDtypeStruct(queries.shape, BF16),
+            jax.ShapeDtypeStruct(queries.shape, BF16),
+            jax.ShapeDtypeStruct(key_proj.shape, BF16),
+            jax.ShapeDtypeStruct(value_proj.shape, BF16),
+        ),
+        in_specs=[
+            pl.BlockSpec((1, rows), lambda g: (0, 0)),
+            pl.BlockSpec((1, *broad[1:]), lambda g: (g, 0, 0, 0)),
+            pl.BlockSpec((1, *narrow), lambda g: (g, 0, 0, 0)),
+        ],
+        out_specs=(wide_block, wide_block, head_block, head_block),
+    )(plan, back, sums)
 
 
 def solution(mesh):

time: 81 us -> 76.6 us (0.946)
  local copies, waits for them, and re-layouts: 5.01 us -> 0 us
    unnamed x10 -> x0, local copies, waits for them, and re-layouts: 5.01 us -> none
    pallas_call x0 -> x1, Pallas kernels: none -> 4.24 us  [on_device(): pl.pallas_call(unpack_kernel, grid=(KV_HEADS,), out_shape=(jax.ShapeDtype...]
    pallas_call x1, Pallas kernels: 75.2 us -> 71.5 us  [on_device(): pl.pallas_call(functools.partial(kernel, n_dp, n_ctx, reach), out_shape=(...]
where the time goes in v2:
time: 76.6 us; the launch traced here: 76.4 us
  Pallas kernels  75.7 us (99%)
    pallas_call x1, Pallas kernels, on_device(): pl.pallas_call(functools.partial(kernel, n_dp, n_ctx, reach), out_shape=(...  71.5 us
    pallas_call x1, Pallas kernels, on_device(): pl.pallas_call(unpack_kernel, grid=(KV_HEADS,), out_shape=(jax.ShapeDtype...  4.24 us

profile of v2, /device:TPU:0, one launch (start us, length us, event | category | flops | bytes accessed | tf_op | source)
XLA Modules:
  0.0 76.4 jit_solution(18120255592934963839)
XLA Ops:
  0.6 71.5 %shard_map.93 = (bf16[4,4,32,2048]{3,2,1,0:T(8,128)(2,1)}, bf16[4,4,32,256]{3,2,1,0:T(8,128)(2,1)}) custom-call(bf16[128,4096]{1,0:T(8,128)(2,1)} %q_ref.1, bf16[128,512]{1,0:T(8,128)(2,1)} %k_ref.1, bf16[128,512]{1,0:T(8,128)(2,1)} %v_ref.1, bf16[128,4096]{1,0:T(8,128)(2,1)} %d_ref.1, s32[1,128]{1,0:T(1,128)} %bitcast.1, s32[1,128]{1,0:T(1,128)} %seg_ref.1), custom_call_target="tpu_custom_call" | custom-call | flops 4831838208 | bytes 4194304 | tf_op jit(solution)/shard_map/pallas_call | solution.py:413
  72.1 4.2 %shard_map.94 = (bf16[128,4096]{1,0:T(8,128)(2,1)}, bf16[128,4096]{1,0:T(8,128)(2,1)}, bf16[128,512]{1,0:T(8,128)(2,1)}, bf16[128,512]{1,0:T(8,128)(2,1)}) custom-call(s32[1,128]{1,0:T(1,128)} %bitcast.2, bf16[4,4,32,2048]{3,2,1,0:T(8,128)(2,1)} %get-tuple-element.6.back_ref, bf16[4,4,32,256]{3,2,1,0:T(8,128)(2,1)} %get-tuple-element.7.sums_ref), custom_call_target="tpu_custom_call" | custom-call | tf_op jit(solution)/shard_map/pallas_call | solution.py:433

commit v3 on v2

--- a/solution.py
+++ b/solution.py
@@ -50,9 +50,9 @@
     n_dp, n_ctx, reach,
     q_ref, k_ref, v_ref, d_ref, plan_ref, seg_ref,
     back, sum_back,
-    kv_out, qd_out, kv, qd, segs, res, own, term_out, term_in, sum_out,
+    q_in, d_in, kv_out, qd_out, kv, qd, segs, res, own, term_out, term_in, sum_out,
     bias, q_cat, d_cat, w_t, ds_t,
-    kv_s, kv_r, qd_s, qd_r, ctx_s, ctx_r, beside_s, seg_s, seg_r, res_s, res_r, term_s, term_r, sum_s, sum_r,
+    fetch_sem, kv_s, kv_r, qd_s, qd_r, ctx_s, ctx_r, beside_s, seg_s, seg_r, res_s, res_r, term_s, term_r, sum_s, sum_r,
 ):
     rows = q_ref.shape[0]
     share = rows // n_dp
@@ -61,6 +61,12 @@
     a = lax.axis_index("dp")
     c = lax.axis_index("ctx")
 
+    fetches = (
+        pltpu.make_async_copy(q_ref, q_in, fetch_sem.at[0]),
+        pltpu.make_async_copy(d_ref, d_in, fetch_sem.at[1]),
+    )
+    for fetch in fetches:
+        fetch.start()
     barrier = pltpu.get_barrier_semaphore()
     for i in range(1, n_dp):
         pl.semaphore_signal(
@@ -72,7 +78,9 @@
         )
 
     def to_dp(src, dst, i, g, send, recv):
-        peer = lax.rem(a + i, n_dp)
+        peer = lax.rem(a + 2 * (i // 2), n_dp)
+        if i % 2:
+            peer = peer + 1 - 2 * lax.rem(peer, 2)
         return pltpu.make_async_remote_copy(
             src_ref=src.at[g, peer],
             dst_ref=dst(g),
@@ -153,7 +161,7 @@
         )
 
     heads = range(KV_HEADS)
-    peers = range(1, n_dp)
+    peers = [*range(2, n_dp), 1]
     hops = range(1, reach + 1)
 
     def has_higher(r):
@@ -185,10 +193,12 @@
         def _():
             seg_copy(r).start()
 
+    for fetch in fetches:
+        fetch.wait()
     for g in heads:
         cols = slice(g * WIDE, (g + 1) * WIDE)
-        qd_out[g, :, :, :WIDE] = packed(q_ref[:, cols])
-        qd_out[g, :, :, WIDE:] = packed(d_ref[:, cols])
+        qd_out[g, :, :, :WIDE] = packed(q_in[:, cols])
+        qd_out[g, :, :, WIDE:] = packed(d_in[:, cols])
         for i in peers:
             qd_copy(g, i).start()
         qd[g, a] = qd_out[g, a]
@@ -379,12 +389,15 @@
     keys = (reach + 1) * rows
     stacked = GROUP * rows
     vmem = pl.BlockSpec(memory_space=pltpu.VMEM)
+    whole = pl.BlockSpec(memory_space=pl.ANY)
     dma = pltpu.SemaphoreType.DMA
     dp_sem = dma((KV_HEADS, n_dp - 1))
     hop_sem = dma((KV_HEADS, reach))
     narrow = (n_dp, share, 2 * HEAD_DIM)
     broad = (KV_HEADS, n_dp, share, 2 * WIDE)
     scratch = [
+        pltpu.VMEM(queries.shape, BF16),
+        pltpu.VMEM(queries.shape, BF16),
         pltpu.VMEM((KV_HEADS, *narrow), BF16),
         pltpu.VMEM(broad, BF16),
         pltpu.VMEM((KV_HEADS, reach + 1, *narrow), BF16),
@@ -400,6 +413,7 @@
         pltpu.VMEM((stacked, HEAD_DIM), BF16),
         pltpu.VMEM((keys, stacked), BF16),
         pltpu.VMEM((keys, stacked), BF16),
+        dma((2,)),
         dp_sem, dp_sem,
         dp_sem, dp_sem,
         hop_sem, hop_sem,
@@ -416,7 +430,7 @@
             jax.ShapeDtypeStruct(broad, BF16),
             jax.ShapeDtypeStruct((KV_HEADS, *narrow), BF16),
         ),
-        in_specs=[vmem] * 6,
+        in_specs=[whole, vmem, vmem, whole, vmem, vmem],
         out_specs=(vmem,) * 2,
         scratch_shapes=scratch,
         compiler_params=pltpu.CompilerParams(

time: 76.6 us -> 76 us (level)
  no operation moved by 1% of the time
where the time goes in v3:
time: 76 us; the launch traced here: 75.8 us
  Pallas kernels  75.1 us (99%)
    pallas_call x1, Pallas kernels, on_device(): pl.pallas_call(functools.partial(kernel, n_dp, n_ctx, reach), out_shape=(...  70.9 us
    pallas_call x1, Pallas kernels, on_device(): pl.pallas_call(unpack_kernel, grid=(KV_HEADS,), out_shape=(jax.ShapeDtype...  4.24 us

profile of v3, /device:TPU:0, one launch (start us, length us, event | category | flops | bytes accessed | tf_op | source)
XLA Modules:
  0.0 75.8 jit_solution(8873293809357825123)
XLA Ops:
  0.6 70.9 %shard_map.93 = (bf16[4,4,32,2048]{3,2,1,0:T(8,128)(2,1)}, bf16[4,4,32,256]{3,2,1,0:T(8,128)(2,1)}) custom-call(bf16[128,4096]{1,0:T(8,128)(2,1)} %q_ref.1, bf16[128,512]{1,0:T(8,128)(2,1)} %k_ref.1, bf16[128,512]{1,0:T(8,128)(2,1)} %v_ref.1, bf16[128,4096]{1,0:T(8,128)(2,1)} %d_ref.1, s32[1,128]{1,0:T(1,128)} %bitcast.1, s32[1,128]{1,0:T(1,128)} %seg_ref.1), custom_call_target="tpu_custom_call" | custom-call | flops 4831838208 | bytes 4194304 | tf_op jit(solution)/shard_map/pallas_call | solution.py:427
  71.5 4.2 %shard_map.94 = (bf16[128,4096]{1,0:T(8,128)(2,1)}, bf16[128,4096]{1,0:T(8,128)(2,1)}, bf16[128,512]{1,0:T(8,128)(2,1)}, bf16[128,512]{1,0:T(8,128)(2,1)}) custom-call(s32[1,128]{1,0:T(1,128)} %bitcast.2, bf16[4,4,32,2048]{3,2,1,0:T(8,128)(2,1)} %get-tuple-element.6.back_ref, bf16[4,4,32,256]{3,2,1,0:T(8,128)(2,1)} %get-tuple-element.7.sums_ref), custom_call_target="tpu_custom_call" | custom-call | tf_op jit(solution)/shard_map/pallas_call | solution.py:447
